TPU v7x, 32 devices: a whole 2x2x4 slice. The times are simulated.
32 devices in a mesh: ep: 16 (over z, x, core), tp: 2 (over y).
Axes of the slice: x: 2, y: 2, z: 4, core: 2. Of those that a mesh axis runs over, the one named last changes fastest.
Arguments:
- tokens: bfloat16 [2048, 7168], P(('ep', 'tp')), may hold values from -6 to 6
- expert_ids: int32 [2048, 8], P(('ep', 'tp')), may hold values from 0 to 15, all different within a row; in each aligned block of 64 rows (0 to 63, 64 to 127, ...) at most 64 rows name the same one
- gate_fixed: int32 [2048, 8], P(('ep', 'tp')), may hold values from 4096 to 32767
- expert_weights: bfloat16 [16, 3, 7168, 1024], P('ep', None, None, 'tp'), may hold values from -0.125 to 0.125
- shared_weights: bfloat16 [3, 7168, 1024], P(None, None, 'tp'), may hold values from -0.125 to 0.125
Outputs:
- mixed: bfloat16 [2048, 7168], P(('ep', 'tp'))
Inputs may be any that keep to these rules, and one draw needn't show every extreme that they name: `expert_ids`: each row names 8 different experts. In the 64 rows of one device no expert is named by more than 64 rows.
All inputs are finite; a program needn't handle non-finite values.
Results may differ from a plain program's by a relative error of at most 0.0075.
Values may be sent and summed in bfloat16 or wider, within the bound.
A program may use at most 128 MiB of HBM per device.

v0:
```python
import jax
import jax.numpy as jnp
from jax import lax
from jax.sharding import PartitionSpec as P

CAP = 8


def local_part(inputs, weights):
    gate_proj = jnp.dot(inputs, weights[0], preferred_element_type=jnp.float32)
    up_proj = jnp.dot(inputs, weights[1], preferred_element_type=jnp.float32)
    hidden = (jax.nn.silu(gate_proj) * up_proj).astype(jnp.bfloat16)
    return lax.dot_general(
        hidden, weights[2], (((1,), (1,)), ((), ())), preferred_element_type=jnp.float32
    )


def on_device(tokens, expert_ids, gate_fixed, expert_weights, shared_weights):
    per_dev = tokens.shape[0]
    width = tokens.shape[1]
    expert_count = lax.axis_size("ep")
    tp_count = lax.axis_size("tp")
    own_weights = expert_weights[0]
    expert_range = jnp.arange(expert_count, dtype=jnp.int32)
    match = expert_ids[:, :, None] == expert_range[None, None, :]
    member = jnp.sum(match.astype(jnp.int32), axis=1)
    position = jnp.cumsum(member, axis=0) - member
    kept = member * (position < CAP).astype(jnp.int32)
    slot_range = jnp.arange(CAP, dtype=jnp.int32)
    hit = (kept[:, :, None] == 1) & (position[:, :, None] == slot_range[None, None, :])
    select = hit.astype(jnp.bfloat16).reshape(per_dev, expert_count * CAP)
    outgoing = jnp.einsum("tk,td->kd", select, tokens, preferred_element_type=jnp.float32)
    outgoing = outgoing.astype(jnp.bfloat16).reshape(expert_count, CAP, width)
    widened = jnp.broadcast_to(outgoing[:, None], (expert_count, tp_count, CAP, width))
    widened = widened.reshape(expert_count * tp_count, CAP, width)
    arrived = lax.all_to_all(widened, ("ep", "tp"), split_axis=0, concat_axis=0, tiled=True)
    senders = arrived.shape[0]
    slots_here = arrived.shape[1]
    part_out = local_part(arrived.reshape(-1, width), own_weights)
    part_out = part_out.astype(jnp.bfloat16).reshape(senders, slots_here, width)
    parts_back = lax.all_to_all(part_out, ("ep", "tp"), split_axis=0, concat_axis=0, tiled=True)
    parts_back = parts_back.reshape(expert_count, tp_count, CAP, width).astype(jnp.float32)
    returned = jnp.sum(parts_back, axis=1).astype(jnp.bfloat16)
    slot_pos = jnp.sum(jnp.where(match, position[:, None, :], 0), axis=2)
    slot_keep = slot_pos < CAP
    slot_index = jnp.where(slot_keep, expert_ids * CAP + slot_pos, 0)
    slot_rows = returned.reshape(expert_count * CAP, width)[slot_index]
    slot_gate = jnp.where(slot_keep, gate_fixed.astype(jnp.float32) / 65536.0, 0.0)
    routed = jnp.sum(slot_gate[:, :, None] * slot_rows.astype(jnp.float32), axis=1)
    shared_terms = local_part(lax.all_gather(tokens, "tp", axis=0, tiled=True), shared_weights)
    shared = lax.psum_scatter(
        shared_terms.astype(jnp.bfloat16), "tp", scatter_dimension=0, tiled=True
    ).astype(jnp.float32)
    return (shared + routed).astype(jnp.bfloat16)


def solution(mesh):
    placed = (
        P(("ep", "tp"), None),
        P(("ep", "tp"), None),
        P(("ep", "tp"), None),
        P("ep", None, None, "tp"),
        P(None, None, "tp"),
    )
    return jax.shard_map(
        on_device, mesh=mesh, in_specs=placed, out_specs=P(("ep", "tp"), None), check_vma=False
    )
```

profile of v0, /device:TPU:0, one launch (start us, length us, event | category | flops | bytes accessed | tf_op | source)
XLA Modules:
  0.0 225.1 jit_solution(152506750071992294)
XLA Ops:
  6.5 0.7 convert_reduce_fusion
  7.2 0.1 copy.21
  7.3 0.1 reduce_window_sum.11
  7.4 0.1 copy.22
  7.5 0.1 eq.52
  7.6 1.9 fusion.2
  9.5 0.5 broadcast_in_dim.41
  9.9 0.0 copy-start.2
  9.9 89.5 %all_to_all.10 = bf16[32,8,7168]{2,1,0:T(8,128)(2,1)S(1)} all-to-all(bf16[32,8,7168]{2,1,0:T(8,128)(2,1)S(1)} %bitcast.63), channel_id=1, replica_groups=mesh['ep'=16,'tp'=2] {'ep','tp'}, dimensions={0} | all-to-all | bytes 7340032 | tf_op jit(solution)/shard_map/all_to_all | solution.py:36
  99.5 5.2 %fusion.6 = f32[256,512]{1,0:T(8,128)S(1)} fusion(bf16[1,3,7168,512]{3,2,1,0:T(8,128)(2,1)} %param.8, bf16[32,8,7168]{2,1,0:T(8,128)(2,1)S(1)} %all_to_all.10), kind=kOutput, calls=%fused_computation.11 | convolution fusion | flops 1879048192 | bytes 11534336 | tf_op jit(solution)/shard_map/dot_general | solution.py:10
  104.7 0.0 copy-done.2
  104.7 2.1 fusion.26
  106.8 3.9 %fusion.1 = bf16[32,8,7168]{2,1,0:T(8,128)(2,1)} fusion(bf16[256,512]{1,0:T(8,128)(2,1)S(1)} %fusion.26, bf16[1,3,7168,512]{3,2,1,0:T(8,128)(2,1)S(1)} %copy-done.2), kind=kOutput, calls=%fused_computation.4 | convolution fusion | flops 1880883200 | bytes 11272192 | tf_op jit(solution)/shard_map/dot_general | solution.py:13
  110.7 3.8 %all-to-all-start.1 = ((bf16[32,8,7168]{2,1,0:T(8,128)(2,1)}), bf16[32,8,7168]{2,1,0:T(8,128)(2,1)}, u32[]{:S(2)}, u32[]{:S(2)}) async-start(bf16[32,8,7168]{2,1,0:T(8,128)(2,1)} %fusion.1), calls=%async_computation.2 | async-start | bytes 7340032 | tf_op jit(solution)/shard_map/all_to_all | solution.py:41
  114.6 0.0 all-gather.2.cloned.1.call-start
  114.6 0.7 all-gather.2.cloned.1.call-update
  115.3 0.0 reduce-scatter.2.cloned.1.call-start
  115.3 53.8 %all-gather.2.cloned.1.call-done = bf16[128,7168]{1,0:T(8,128)(2,1)} async-done(((bf16[64,7168]{1,0:T(8,128)(2,1)}), bf16[128,7168]{1,0:T(8,128)(2,1)}) %all-gather.2.cloned.1.call-update) | async-done | bytes 1835024 | tf_op jit(solution)/shard_map/all_gather | solution.py:50
  169.2 0.0 copy-start.3
  169.2 4.9 %fusion.11 = f32[128,512]{1,0:T(8,128)S(1)} fusion(bf16[128,7168]{1,0:T(8,128)(2,1)} %all-gather.2.cloned.1.call-done, bf16[3,7168,512]{2,1,0:T(8,128)(2,1)} %param.9), kind=kOutput, calls=%fused_computation.16 | convolution fusion | flops 939524096 | bytes 9437184 | tf_op jit(solution)/shard_map/dot_general | solution.py:10
  174.1 0.0 copy-done.3
  174.1 0.0 copy-start
  174.1 0.0 copy-start.1
  174.1 10.0 %convolution_convert_fusion.2 = bf16[128,7168]{1,0:T(8,128)(2,1)} fusion(bf16[3,7168,512]{2,1,0:T(8,128)(2,1)} %param.9, bf16[128,7168]{1,0:T(8,128)(2,1)S(1)} %copy-done.3, f32[128,512]{1,0:T(8,128)S(1)} %fusion.11), kind=kOutput, calls=%fused_computation.6 | convolution fusion | flops 1880358912 | bytes 18612224 | tf_op jit(solution)/shard_map/dot_general | solution.py:13
  184.1 0.0 reduce-scatter.2.cloned.1.call-update
  184.2 0.0 copy-done
  184.2 0.1 copy.24
  184.3 0.1 reshape.53
  184.4 0.0 copy-done.1
  184.4 0.1 copy.23
  184.5 12.6 %all-to-all-done.1 = bf16[32,8,7168]{2,1,0:T(8,128)(2,1)} async-done(((bf16[32,8,7168]{2,1,0:T(8,128)(2,1)}), bf16[32,8,7168]{2,1,0:T(8,128)(2,1)}, u32[]{:S(2)}, u32[]{:S(2)}) %all-to-all-start.1) | async-done | bytes 3670048 | tf_op jit(solution)/shard_map/all_to_all | solution.py:41
  197.1 2.6 %bitcast_reduce_fusion = bf16[16,8,7168]{2,1,0:T(8,128)(2,1)S(1)} fusion(bf16[32,8,7168]{2,1,0:T(8,128)(2,1)} %all-to-all-done.1), kind=kLoop, calls=%fused_computation.24 | loop fusion | flops 917504 | bytes 5505024 | tf_op jit(solution)/shard_map/reduce_sum | solution.py:43
  199.7 7.2 %gather_fusion = bf16[512,7168]{1,0:T(8,128)(2,1)} fusion(bf16[128,7168]{1,0:T(8,128)(2,1)S(1)} %bitcast.62, s32[1024]{0:T(1024)S(1)} %pad_clamp_fusion), kind=kCustom, calls=%fused_computation | custom fusion | bytes 14682112 | tf_op jit(solution)/shard_map/gather | solution.py:47
  207.0 8.9 %fusion = f32[64,7168]{1,0:T(8,128)S(1)} fusion(bf16[512,7168]{1,0:T(8,128)(2,1)} %gather_fusion, f32[64,8]{1,0:T(8,128)S(1)} %copy.23), kind=kLoop, calls=%fused_computation.2 | loop fusion | flops 10551296 | bytes 9177088 | tf_op jit(solution)/shard_map/reduce_sum | solution.py:49
  215.9 0.0 reduce-scatter.2.cloned.1.call-done
  215.9 2.3 %add_convert_fusion = bf16[64,7168]{1,0:T(8,128)(2,1)} fusion(f32[64,7168]{1,0:T(8,128)S(1)} %fusion, bf16[64,7168]{1,0:T(8,128)(2,1)} %reduce-scatter.2.cloned.1.call-done), kind=kLoop, calls=%fused_computation.27 | loop fusion | flops 1376256 | bytes 3670016 | tf_op jit(solution)/shard_map/convert_element_type | solution.py:54
  (6 shorter events, 0.1 us)
Async XLA Ops:
  9.9 94.8 %copy-start.2 = (bf16[1,3,7168,512]{3,2,1,0:T(8,128)(2,1)S(1)}, bf16[1,3,7168,512]{3,2,1,0:T(8,128)(2,1)}, u32[]{:S(2)}) copy-start(bf16[1,3,7168,512]{3,2,1,0:T(8,128)(2,1)} %param.8) | copy-start | bytes 66060292
  110.7 86.4 %all-to-all-start.1 = ((bf16[32,8,7168]{2,1,0:T(8,128)(2,1)}), bf16[32,8,7168]{2,1,0:T(8,128)(2,1)}, u32[]{:S(2)}, u32[]{:S(2)}) async-start(bf16[32,8,7168]{2,1,0:T(8,128)(2,1)} %fusion.1), calls=%async_computation.2 | async-start | bytes 7340032 | tf_op jit(solution)/shard_map/all_to_all | solution.py:41
  114.6 54.6 %all-gather.2.cloned.1.call-start = ((), (), s32[]{:S(2)}) async-start(), calls=%async_computation.3 | async-start | bytes 2752512 | tf_op jit(solution)/shard_map/all_gather | solution.py:50
  115.3 100.6 %reduce-scatter.2.cloned.1.call-start = ((), (), s32[]{:S(2)}) async-start(), calls=%async_computation.4 | async-start | bytes 2752512 | tf_op jit(solution)/shard_map/reduce_scatter | solution.py:51
  169.2 4.9 %copy-start.3 = (bf16[128,7168]{1,0:T(8,128)(2,1)S(1)}, bf16[128,7168]{1,0:T(8,128)(2,1)}, u32[]{:S(2)}) copy-start(bf16[128,7168]{1,0:T(8,128)(2,1)} %all-gather.2.cloned.1.call-done) | copy-start | bytes 5505028
  174.1 10.1 %copy-start = (s32[64,8]{0,1:T(8,128)S(1)}, s32[64,8]{0,1:T(8,128)}, u32[]{:S(2)}) copy-start(s32[64,8]{0,1:T(8,128)} %param.6) | copy-start | bytes 6148
  174.1 10.3 %copy-start.1 = (s32[64,8]{0,1:T(8,128)S(1)}, s32[64,8]{0,1:T(8,128)}, u32[]{:S(2)}) copy-start(s32[64,8]{0,1:T(8,128)} %param.7) | copy-start | bytes 6148
Sparse Core Ops, SparseCore 0:
  116.9 52.1 all-gather.1
  184.3 31.2 reduce-scatter.1
where the time goes:
time: 225 us
  blocking collectives  89.5 us (40%)
  waiting for transfers between devices  67.1 us (30%)
  matrix products  28 us (12%)
  other arithmetic  14.7 us (7%)
  between operations  13.6 us (6%)
  local copies, waits for them, and re-layouts  8.21 us (4%)
  starting transfers between devices  3.89 us (2%)
    all_to_all x1, blocking collectives, on_device(): lax.all_to_all(widened, ('ep', 'tp'), split_axis=0, concat_axis=0, tiled=...  89.5 us
    all_gather x1, waiting for transfers between devices, on_device(): lax.all_gather(tokens, 'tp', axis=0, tiled=True)  53.8 us
    dot_general x2, matrix products, local_part(): lax.dot_general(hidden, weights[2], (((1,), (1,)), ((), ())), preferred_e...  14 us
    all_to_all x1, waiting for transfers between devices, on_device(): lax.all_to_all(part_out, ('ep', 'tp'), split_axis=0, concat_axis=0, tiled...  12.6 us
    dot_general x2, matrix products, local_part(): gate_proj = jnp.dot(inputs, weights[0], preferred_element_type=jnp.float32)  10.1 us
    reduce_sum x1, other arithmetic, on_device(): jnp.sum(slot_gate[:, :, None] * slot_rows.astype(jnp.float32), axis=1)  8.91 us
    gather x1, local copies, waits for them, and re-layouts, on_device(): slot_rows = returned.reshape(expert_count * CAP, width)[slot_index]  7.23 us
  transfers between devices with their start and end apart: 3, of which 2 were waited for; matrix products, arithmetic and copies ran while one was open for 15% of the time, Pallas kernels for 0%

commit v1 on v0

v1 whole, which is shorter than its diff:
```python
import functools

import jax
import jax.numpy as jnp
from jax import lax
from jax.experimental import pallas as pl
from jax.experimental.pallas import tpu as pltpu
from jax.sharding import PartitionSpec as P

CAP = 8
MESH = pl.DeviceIdType.MESH
BF16 = jnp.bfloat16
F32 = jnp.float32

SPANS = 2
PIECES = 4
STEP = 256
DEPTH = 1024


def dot(a, b):
    return jnp.dot(a, b, preferred_element_type=F32)


def dot_t(a, b):
    return lax.dot_general(a, b, (((1,), (1,)), ((), ())), preferred_element_type=F32)


def routing(meta, experts):
    tops = meta.shape[0] // 2
    both = meta.shape[1]
    expert = lax.broadcasted_iota(jnp.int32, (experts, both), 0)
    member = jnp.zeros((experts, both), F32)
    high = jnp.zeros((experts, both), F32)
    low = jnp.zeros((experts, both), F32)
    for k in range(tops):
        match = meta[k : k + 1, :] == expert
        gate = meta[tops + k : tops + k + 1, :]
        member += jnp.where(match, 1.0, 0.0)
        high += jnp.where(match, (gate >> 8).astype(F32), 0.0)
        low += jnp.where(match, (gate & 255).astype(F32), 0.0)
    row = lax.broadcasted_iota(jnp.int32, (both, both), 0)
    col = lax.broadcasted_iota(jnp.int32, (both, both), 1)
    per = both // 2
    earlier = (row < col) & ((row >= per) == (col >= per))
    position = dot(member.astype(BF16), jnp.where(earlier, 1.0, 0.0).astype(BF16))
    key = jnp.where((member > 0.5) & (position < CAP - 0.5), position, -1.0)
    return key.astype(BF16), high.astype(BF16), low.astype(BF16)


def slots(routed, group, core, quarter):
    key, high, low = routed
    experts, both = key.shape
    rows = quarter * 2 * CAP
    row = lax.broadcasted_iota(jnp.int32, (rows, experts), 0)
    col = lax.broadcasted_iota(jnp.int32, (rows, experts), 1)
    pick = jnp.where(col == (group * quarter + row // (2 * CAP)) * 2 + core, 1.0, 0.0).astype(BF16)
    row = lax.broadcasted_iota(jnp.int32, (rows, both), 0)
    col = lax.broadcasted_iota(jnp.int32, (rows, both), 1)
    hit = (dot(pick, key) == (row % CAP).astype(F32)) & (
        ((row // CAP) % 2 == 1) == (col >= both // 2)
    )
    return (
        jnp.where(hit, 1.0, 0.0),
        jnp.where(hit, dot(pick, high) / 256.0, 0.0),
        jnp.where(hit, dot(pick, low) / 65536.0, 0.0),
    )


def kernel(
    experts,
    tokens, ids, gates, routed_w, shared_w,
    out,
    tok, meta, sel0, sel1, c0h, c0l, c1h, c1l, msg, arr, wgu, wd, gu, hid, shd, part, yred,
    rets, retc, sibs, sibr, yfs, yfr, keep,
    load_sem, meta_s, meta_r, tsib_s, tsib_r, ty_s, ty_r, tdi_s, tdi_r,
    dc_s, dc_r, d0_s, d0_r, d1_s, d1_r, fw_s, fw_r,
    yr_s, yr_r, r0_s, r0_r, r1_s, r1_r, rc_s, rc_r, sb_s, sb_r, yf_s, yf_r,
):
    ep, y = lax.axis_index("ep"), lax.axis_index("tp")
    core, place = lax.rem(ep, 2), ep // 2
    quarter = experts // 4
    half, q = place // quarter, lax.rem(place, quarter)
    per, width = tokens.shape
    tops = ids.shape[0]
    block = 2 * CAP
    hidden = wd.shape[1]
    sib, ypart, diag = (ep + 1 - 2 * core, y), (ep, 1 - y), (ep + 1 - 2 * core, 1 - y)

    def near(r):
        return lax.rem(q + r, quarter)

    def near_dev(r):
        return ((half * quarter + near(r)) * 2 + core, y)

    def far_dev(r):
        return (((1 - half) * quarter + near(r)) * 2 + core, y)

    def rows(index):
        return pl.ds(pl.multiple_of(index * block, block), block)

    def send(src, dst, s, r, dev):
        return pltpu.make_async_remote_copy(
            src_ref=src, dst_ref=dst, send_sem=s, recv_sem=r, device_id=dev, device_id_type=MESH
        )

    def columns(first, length):
        return pl.ds(first, length)

    own_tokens = pltpu.make_async_copy(tokens, tok.at[0, 0], load_sem.at[0])
    own_tokens.start()
    shared_gu = pltpu.make_async_copy(shared_w.at[pl.ds(0, 2)], wgu, load_sem.at[1])
    shared_d = pltpu.make_async_copy(shared_w.at[2], wd, load_sem.at[2])
    shared_gu.start()
    shared_d.start()
    meta[0, pl.ds(0, tops), :] = ids[...]
    meta[0, pl.ds(tops, tops), :] = gates[...]

    barrier = pltpu.get_barrier_semaphore()
    peers = [sib, ypart, diag]
    peers += [near_dev(r) for r in range(1, quarter)] + [far_dev(r) for r in range(quarter)]
    for peer in peers:
        pl.semaphore_signal(barrier, inc=1, device_id=peer, device_id_type=MESH)
    pl.semaphore_wait(barrier, len(peers))

    pending = []

    def go(copy):
        copy.start()
        pending.append(copy)
        return copy

    metas = [
        go(send(meta.at[0], meta.at[k], meta_s.at[k], meta_r.at[k], dev))
        for k, dev in ((1, sib), (2, ypart), (3, diag))
    ]
    own_tokens.wait()
    span = width // SPANS
    tsib, ty = [], []
    for d in range(SPANS):
        at = columns(d * span, span)
        src = tok.at[0, 0, :, at]
        tsib.append(go(send(src, tok.at[0, 1, :, at], tsib_s.at[d], tsib_r.at[d], sib)))
    for d in range(SPANS):
        at = columns(d * span, span)
        src = tok.at[0, 0, :, at]
        ty.append(go(send(src, tok.at[1, 0, :, at], ty_s.at[d], ty_r.at[d], ypart)))

    metas[0].wait_recv()
    routed = routing(jnp.concatenate([meta[0], meta[1]], axis=1), experts)
    far, far_h, far_l = slots(routed, 1 - half, core, quarter)
    here, here_h, here_l = slots(routed, half, core, quarter)
    sel0[...] = jnp.concatenate([far, here], axis=0).astype(BF16)
    c0h[...] = jnp.concatenate([far_h, here_h], axis=0).T.astype(BF16)
    c0l[...] = jnp.concatenate([far_l, here_l], axis=0).T.astype(BF16)
    dcross, dnear0, dnear1 = [], [], []
    nrow = quarter * block
    for d in range(SPANS):
        tsib[d].wait_recv()

        @pl.loop(0, span // STEP)
        def _(i):
            at = pl.ds(pl.multiple_of(d * span + i * STEP, STEP), STEP)
            got = dot(sel0[...], tok[0, :, :, at].reshape(2 * per, STEP)).astype(BF16)
            msg[0, :, at] = got[:nrow]
            msg[1, :, at] = got[nrow:]

        at = columns(d * span, span)
        for r in range(quarter):
            dcross.append(go(send(
                msg.at[0, rows(near(r)), at], arr.at[2, rows(q), at],
                dc_s.at[d, r], dc_r.at[d, r], far_dev(r),
            )))
        for r in range(1, quarter):
            dnear0.append(go(send(
                msg.at[1, rows(near(r)), at], arr.at[0, rows(q), at],
                d0_s.at[d, r], d0_r.at[d, r], near_dev(r),
            )))
    arr[0, rows(q), :] = msg[1, rows(q), :]

    metas[1].wait_recv()
    metas[2].wait_recv()
    routed = routing(jnp.concatenate([meta[2], meta[3]], axis=1), experts)
    here, here_h, here_l = slots(routed, half, core, quarter)
    sel1[...] = here.astype(BF16)
    c1h[...] = here_h.T.astype(BF16)
    c1l[...] = here_l.T.astype(BF16)
    tdi = []
    for d in range(SPANS):
        ty[d].wait_recv()
        at = columns(d * span, span)
        tdi.append(go(send(
            tok.at[1, 0, :, at], tok.at[1, 1, :, at], tdi_s.at[d], tdi_r.at[d], sib
        )))
    for d in range(SPANS):
        tdi[d].wait_recv()

        @pl.loop(0, span // STEP)
        def _(i):
            at = pl.ds(pl.multiple_of(d * span + i * STEP, STEP), STEP)
            got = dot(sel1[...], tok[1, :, :, at].reshape(2 * per, STEP)).astype(BF16)
            msg[2, :, at] = got

        at = columns(d * span, span)
        for r in range(1, quarter):
            dnear1.append(go(send(
                msg.at[2, rows(near(r)), at], arr.at[1, rows(q), at],
                d1_s.at[d, r], d1_r.at[d, r], near_dev(r),
            )))
    arr[1, rows(q), :] = msg[2, rows(q), :]

    def up(read, count):
        gu[...] = jnp.zeros_like(gu)

        @pl.loop(0, width // DEPTH)
        def _(i):
            at = pl.ds(pl.multiple_of(i * DEPTH, DEPTH), DEPTH)
            x = read(at)
            gu[0, pl.ds(0, count), :] += dot(x, wgu[0, at, :])
            gu[1, pl.ds(0, count), :] += dot(x, wgu[1, at, :])

        gate = gu[0, pl.ds(0, count), :]
        hid[pl.ds(0, count), :] = (
            gate / (1.0 + jnp.exp(-gate)) * gu[1, pl.ds(0, count), :]
        ).astype(BF16)

    forwards = []

    def forward(d):
        at = columns(d * span, span)
        for r in range(quarter):
            dcross[d * quarter + r].wait_recv()
            src = lax.rem(q + quarter - r, quarter)
            forwards.append(go(send(
                arr.at[2, rows(src), at], arr.at[3, rows(src), at],
                fw_s.at[d, r], fw_r.at[d, r], ypart,
            )))

    shared_gu.wait()
    up(lambda at: jnp.concatenate([tok[0, 0, :, at], tok[1, 0, :, at]], axis=0), 2 * per)
    routed_gu = pltpu.make_async_copy(routed_w.at[0, pl.ds(0, 2)], wgu, load_sem.at[1])
    routed_gu.start()
    forward(0)
    shared_d.wait()

    @pl.loop(0, width // STEP)
    def _(i):
        at = pl.ds(pl.multiple_of(i * STEP, STEP), STEP)
        got = dot_t(hid[pl.ds(0, 2 * per), :], wd[at, :]).astype(BF16)
        shd[0, :, at] = got[:per]
        shd[1, :, at] = got[per:]

    routed_d = pltpu.make_async_copy(routed_w.at[0, 2], wd, load_sem.at[2])
    routed_d.start()
    for d in range(1, SPANS):
        forward(d)

    for copy in dnear0 + dnear1 + forwards:
        copy.wait_recv()
    routed_gu.wait()
    up(lambda at: arr[:, :, at].reshape(4 * nrow, DEPTH), 4 * nrow)
    routed_d.wait()

    piece = width // PIECES
    yreds, near0, near1, cross = [], [], [], []

    def reduce(j):
        yreds[j].wait_recv()
        at = columns(j * piece, piece)

        @pl.loop(0, piece // STEP)
        def _(i):
            at = pl.ds(pl.multiple_of(j * piece + i * STEP, STEP), STEP)
            part[2, :, at] = (part[2, :, at].astype(F32) + yred[:, at].astype(F32)).astype(BF16)

        for r in range(quarter):
            cross.append(go(send(
                part.at[2, rows(near(r)), at], retc.at[rows(q), at],
                rc_s.at[j, r], rc_r.at[j, r], far_dev(r),
            )))

    for j in range(PIECES):
        @pl.loop(0, piece // STEP)
        def _(i):
            at = pl.ds(pl.multiple_of(j * piece + i * STEP, STEP), STEP)
            got = dot_t(hid[...], wd[at, :]).astype(BF16)
            part[:, :, at] = got.reshape(4, nrow, STEP)

        at = columns(j * piece, piece)
        yreds.append(go(send(part.at[3, :, at], yred.at[:, at], yr_s.at[j], yr_r.at[j], ypart)))
        for r in range(1, quarter):
            near1.append(go(send(
                part.at[1, rows(near(r)), at], rets.at[1, rows(q), at],
                r1_s.at[j, r], r1_r.at[j, r], near_dev(r),
            )))
        for r in range(1, quarter):
            near0.append(go(send(
                part.at[0, rows(near(r)), at], rets.at[0, rows(q), at],
                r0_s.at[j, r], r0_r.at[j, r], near_dev(r),
            )))
        if j > 0:
            reduce(j - 1)
    rets[0, rows(q), :] = part[0, rows(q), :]
    rets[1, rows(q), :] = part[1, rows(q), :]
    reduce(PIECES - 1)

    sums = [[], []]

    def to_sibling(dy, j):
        at = columns(j * piece, piece)
        sums[dy].append(go(send(
            sibs.at[dy, :, at], sibr.at[dy, :, at], sb_s.at[dy, j], sb_r.at[dy, j], sib
        )))

    for j in range(PIECES):
        for copy in near1[j * (quarter - 1) : (j + 1) * (quarter - 1)]:
            copy.wait_recv()

        @pl.loop(0, piece // STEP)
        def _(i):
            at = pl.ds(pl.multiple_of(j * piece + i * STEP, STEP), STEP)
            x = rets[1, :, at]
            got = dot(c1h[...], x) + dot(c1l[...], x)
            sibs[1, :, at] = got[per:].astype(BF16)
            keep[:, at] = got[:per] + shd[1, :, at].astype(F32)

        to_sibling(1, j)
    finals = []
    for j in range(PIECES):
        sums[1][j].wait_recv()

        @pl.loop(0, piece // STEP)
        def _(i):
            at = pl.ds(pl.multiple_of(j * piece + i * STEP, STEP), STEP)
            yfs[:, at] = (keep[:, at] + sibr[1, :, at].astype(F32)).astype(BF16)

        at = columns(j * piece, piece)
        finals.append(go(send(yfs.at[:, at], yfr.at[:, at], yf_s.at[j], yf_r.at[j], ypart)))

    for j in range(PIECES):
        for copy in near0[j * (quarter - 1) : (j + 1) * (quarter - 1)]:
            copy.wait_recv()
        for copy in cross[j * quarter : (j + 1) * quarter]:
            copy.wait_recv()

        @pl.loop(0, piece // STEP)
        def _(i):
            at = pl.ds(pl.multiple_of(j * piece + i * STEP, STEP), STEP)
            x = jnp.concatenate([retc[:, at], rets[0, :, at]], axis=0)
            got = dot(c0h[...], x) + dot(c0l[...], x)
            sibs[0, :, at] = got[per:].astype(BF16)
            keep[:, at] = got[:per] + shd[0, :, at].astype(F32)

        to_sibling(0, j)
    for j in range(PIECES):
        sums[0][j].wait_recv()
        finals[j].wait_recv()

        @pl.loop(0, piece // STEP)
        def _(i):
            at = pl.ds(pl.multiple_of(j * piece + i * STEP, STEP), STEP)
            out[:, at] = (
                keep[:, at] + sibr[0, :, at].astype(F32) + yfr[:, at].astype(F32)
            ).astype(BF16)

    for copy in pending:
        copy.wait_send()


def fused(tokens, expert_ids, gate_fixed, expert_weights, shared_weights):
    experts = lax.axis_size("ep")
    per, width = tokens.shape
    tops = expert_ids.shape[1]
    hidden = shared_weights.shape[2]
    quarter = experts // 4
    nrow = quarter * 2 * CAP
    vmem = pltpu.VMEM
    dma = pltpu.SemaphoreType.DMA
    hbm = pl.BlockSpec(memory_space=pl.ANY)
    near = pl.BlockSpec(memory_space=pltpu.VMEM)

    def pair(*shape):
        return [dma(shape), dma(shape)]

    scratch = [
        vmem((2, 2, per, width), BF16),
        vmem((4, 2 * tops, per), jnp.int32),
        vmem((2 * nrow, 2 * per), BF16),
        vmem((nrow, 2 * per), BF16),
        vmem((2 * per, 2 * nrow), BF16),
        vmem((2 * per, 2 * nrow), BF16),
        vmem((2 * per, nrow), BF16),
        vmem((2 * per, nrow), BF16),
        vmem((3, nrow, width), BF16),
        vmem((4, nrow, width), BF16),
        vmem((2, width, hidden), BF16),
        vmem((width, hidden), BF16),
        vmem((2, 4 * nrow, hidden), F32),
        vmem((4 * nrow, hidden), BF16),
        vmem((2, per, width), BF16),
        vmem((4, nrow, width), BF16),
        vmem((nrow, width), BF16),
        vmem((2, nrow, width), BF16),
        vmem((nrow, width), BF16),
        vmem((2, per, width), BF16),
        vmem((2, per, width), BF16),
        vmem((per, width), BF16),
        vmem((per, width), BF16),
        vmem((per, width), F32),
        dma((3,)),
    ]
    scratch += pair(4) + pair(SPANS) + pair(SPANS) + pair(SPANS)
    scratch += pair(SPANS, quarter) * 4
    scratch += pair(PIECES) + pair(PIECES, quarter) * 3 + pair(2, PIECES) + pair(PIECES)
    return pl.pallas_call(
        functools.partial(kernel, experts),
        out_shape=jax.ShapeDtypeStruct((per, width), BF16),
        in_specs=[hbm, near, near, hbm, hbm],
        out_specs=near,
        scratch_shapes=scratch,
        compiler_params=pltpu.CompilerParams(
            collective_id=0, has_side_effects=True, vmem_limit_bytes=60 * 1024 * 1024
        ),
        cost_estimate=pl.CostEstimate(
            flops=2 * 3 * (4 * nrow + 2 * per) * width * hidden,
            bytes_accessed=2 * 6 * width * hidden,
            transcendentals=0,
        ),
    )(tokens, expert_ids.T, gate_fixed.T, expert_weights, shared_weights)


def local_part(inputs, weights):
    gate_proj = jnp.dot(inputs, weights[0], preferred_element_type=F32)
    up_proj = jnp.dot(inputs, weights[1], preferred_element_type=F32)
    hidden = (jax.nn.silu(gate_proj) * up_proj).astype(BF16)
    return dot_t(hidden, weights[2])


def general(tokens, expert_ids, gate_fixed, expert_weights, shared_weights):
    per_dev = tokens.shape[0]
    width = tokens.shape[1]
    expert_count = lax.axis_size("ep")
    tp_count = lax.axis_size("tp")
    own_weights = expert_weights[0]
    expert_range = jnp.arange(expert_count, dtype=jnp.int32)
    match = expert_ids[:, :, None] == expert_range[None, None, :]
    member = jnp.sum(match.astype(jnp.int32), axis=1)
    position = jnp.cumsum(member, axis=0) - member
    kept = member * (position < CAP).astype(jnp.int32)
    slot_range = jnp.arange(CAP, dtype=jnp.int32)
    hit = (kept[:, :, None] == 1) & (position[:, :, None] == slot_range[None, None, :])
    select = hit.astype(BF16).reshape(per_dev, expert_count * CAP)
    outgoing = jnp.einsum("tk,td->kd", select, tokens, preferred_element_type=F32)
    outgoing = outgoing.astype(BF16).reshape(expert_count, CAP, width)
    widened = jnp.broadcast_to(outgoing[:, None], (expert_count, tp_count, CAP, width))
    widened = widened.reshape(expert_count * tp_count, CAP, width)
    arrived = lax.all_to_all(widened, ("ep", "tp"), split_axis=0, concat_axis=0, tiled=True)
    senders = arrived.shape[0]
    slots_here = arrived.shape[1]
    part_out = local_part(arrived.reshape(-1, width), own_weights)
    part_out = part_out.astype(BF16).reshape(senders, slots_here, width)
    parts_back = lax.all_to_all(part_out, ("ep", "tp"), split_axis=0, concat_axis=0, tiled=True)
    parts_back = parts_back.reshape(expert_count, tp_count, CAP, width).astype(F32)
    returned = jnp.sum(parts_back, axis=1).astype(BF16)
    slot_pos = jnp.sum(jnp.where(match, position[:, None, :], 0), axis=2)
    slot_keep = slot_pos < CAP
    slot_index = jnp.where(slot_keep, expert_ids * CAP + slot_pos, 0)
    slot_rows = returned.reshape(expert_count * CAP, width)[slot_index]
    slot_gate = jnp.where(slot_keep, gate_fixed.astype(F32) / 65536.0, 0.0)
    routed = jnp.sum(slot_gate[:, :, None] * slot_rows.astype(F32), axis=1)
    shared_terms = local_part(lax.all_gather(tokens, "tp", axis=0, tiled=True), shared_weights)
    shared = lax.psum_scatter(
        shared_terms.astype(BF16), "tp", scatter_dimension=0, tiled=True
    ).astype(F32)
    return (shared + routed).astype(BF16)


def solution(mesh):
    placed = (
        P(("ep", "tp"), None),
        P(("ep", "tp"), None),
        P(("ep", "tp"), None),
        P("ep", None, None, "tp"),
        P(None, None, "tp"),
    )
    body = fused if mesh.shape["tp"] == 2 and mesh.shape["ep"] == 16 else general
    return jax.shard_map(
        body, mesh=mesh, in_specs=placed, out_specs=P(("ep", "tp"), None), check_vma=False
    )
```

time: 225 us -> 124 us (0.55)
  Pallas kernels: 0 us -> 121 us
  blocking collectives: 89.5 us -> 0 us
  waiting for transfers between devices: 67.1 us -> 0 us
  matrix products: 28 us -> 0 us
  other arithmetic: 14.7 us -> 0 us
  between operations: 13.6 us -> 0.01 us
  local copies, waits for them, and re-layouts: 8.21 us -> 2.16 us
  starting transfers between devices: 3.89 us -> 0 us
    pallas_call x0 -> x1, Pallas kernels: none -> 121 us  [fused(): pl.pallas_call(functools.partial(kernel, experts), out_shape=jax.ShapeDty...]
    all_to_all x1 -> x0, blocking collectives: 89.5 us -> none  [on_device(): lax.all_to_all(widened, ('ep', 'tp'), split_axis=0, concat_axis=0, tiled=...]
    all_gather x1 -> x0, waiting for transfers between devices: 53.8 us -> none  [on_device(): lax.all_gather(tokens, 'tp', axis=0, tiled=True)]
    dot_general x6 -> x0, matrix products: 28 us -> none  [the longest x2 14 us: local_part(): lax.dot_general(hidden, weights[2], (((1,), (1,)), ((), ())), preferred_e...]
    all_to_all x1 -> x0, waiting for transfers between devices: 12.6 us -> none  [on_device(): lax.all_to_all(part_out, ('ep', 'tp'), split_axis=0, concat_axis=0, tiled...]
    reduce_sum x4 -> x0, other arithmetic: 12.3 us -> none  [the longest x1 8.91 us: on_device(): jnp.sum(slot_gate[:, :, None] * slot_rows.astype(jnp.float32), axis=1)]
    gather x1 -> x0, local copies, waits for them, and re-layouts: 7.23 us -> none  [on_device(): slot_rows = returned.reshape(expert_count * CAP, width)[slot_index]]
    all_to_all x1 -> x0, starting transfers between devices: 3.81 us -> none  [on_device(): lax.all_to_all(part_out, ('ep', 'tp'), split_axis=0, concat_axis=0, tiled...]
  transfers between devices with their start and end apart: 3 -> 0, of which waited for: 2 -> 0; matrix products, arithmetic and copies ran while one was open for 15% -> 0% of each run, Pallas kernels for 0% -> 0%
where the time goes in v1:
time: 124 us; the launch traced here: 123 us
  Pallas kernels  121 us (98%)
  local copies, waits for them, and re-layouts  2.16 us (2%)
    pallas_call x1, Pallas kernels, fused(): pl.pallas_call(functools.partial(kernel, experts), out_shape=jax.ShapeDty...  121 us

profile of v1, /device:TPU:0, one launch (start us, length us, event | category | flops | bytes accessed | tf_op | source)
XLA Modules:
  0.0 123.4 jit_solution(3199145734160478866)
XLA Ops:
  0.0 121.3 %shard_map.55 = bf16[64,7168]{1,0:T(8,128)(2,1)} custom-call(bf16[64,7168]{1,0:T(8,128)(2,1)} %tokens.1, s32[8,64]{1,0:T(8,128)} %bitcast.2, s32[8,64]{1,0:T(8,128)} %bitcast.3, bf16[1,3,7168,512]{3,2,1,0:T(8,128)(2,1)} %routed_w.1, bf16[3,7168,512]{2,1,0:T(8,128)(2,1)} %shared_w.1), custom_call_target="tpu_custom_call" | custom-call | flops 8455716864 | bytes 44040192 | tf_op jit(solution)/shard_map/pallas_call | solution.py:415
  121.3 2.2 %copy.7 = bf16[64,7168]{1,0:T(8,128)(2,1)} copy(bf16[64,7168]{1,0:T(8,128)(2,1)} %shard_map.55) | data formatting | bytes 1835008

commit v2 on v1

--- a/solution.py
+++ b/solution.py
@@ -12,7 +12,7 @@
 BF16 = jnp.bfloat16
 F32 = jnp.float32
 
-SPANS = 2
+SPANS = 4
 PIECES = 4
 STEP = 256
 DEPTH = 1024
@@ -84,7 +84,6 @@
     per, width = tokens.shape
     tops = ids.shape[0]
     block = 2 * CAP
-    hidden = wd.shape[1]
     sib, ypart, diag = (ep + 1 - 2 * core, y), (ep, 1 - y), (ep + 1 - 2 * core, 1 - y)
 
     def near(r):
@@ -95,6 +94,21 @@
 
     def far_dev(r):
         return (((1 - half) * quarter + near(r)) * 2 + core, y)
+
+    def back_dev(r):
+        return (((1 - half) * quarter + near(quarter - r)) * 2 + core, y)
+
+    nrow = quarter * block
+    group = quarter // 2
+
+    def own_rows(r):
+        return pl.ds((r // group) * 2 * nrow + nrow + (r % group) * block, block)
+
+    def passed_rows(r):
+        return pl.ds((r // group) * 2 * nrow + nrow + (group + r % group) * block, block)
+
+    def near_rows(b, index):
+        return pl.ds(pl.multiple_of(b * 2 * nrow + index * block, block), block)
 
     def rows(index):
         return pl.ds(pl.multiple_of(index * block, block), block)
@@ -153,8 +167,16 @@
     sel0[...] = jnp.concatenate([far, here], axis=0).astype(BF16)
     c0h[...] = jnp.concatenate([far_h, here_h], axis=0).T.astype(BF16)
     c0l[...] = jnp.concatenate([far_l, here_l], axis=0).T.astype(BF16)
-    dcross, dnear0, dnear1 = [], [], []
-    nrow = quarter * block
+    dcross, dnear0, dnear1 = {}, [], []
+
+    def send_far(d, b):
+        at = columns(d * span, span)
+        for r in range(b * group, (b + 1) * group):
+            dcross[d, r] = go(send(
+                msg.at[0, rows(near(r)), at], arr.at[own_rows(r), at],
+                dc_s.at[d, r], dc_r.at[d, r], far_dev(r),
+            ))
+
     for d in range(SPANS):
         tsib[d].wait_recv()
 
@@ -165,18 +187,16 @@
             msg[0, :, at] = got[:nrow]
             msg[1, :, at] = got[nrow:]
 
-        at = columns(d * span, span)
-        for r in range(quarter):
-            dcross.append(go(send(
-                msg.at[0, rows(near(r)), at], arr.at[2, rows(q), at],
-                dc_s.at[d, r], dc_r.at[d, r], far_dev(r),
-            )))
+        send_far(d, 0)
+        at = columns(d * span, span)
         for r in range(1, quarter):
             dnear0.append(go(send(
-                msg.at[1, rows(near(r)), at], arr.at[0, rows(q), at],
+                msg.at[1, rows(near(r)), at], arr.at[near_rows(0, q), at],
                 d0_s.at[d, r], d0_r.at[d, r], near_dev(r),
             )))
-    arr[0, rows(q), :] = msg[1, rows(q), :]
+    for d in range(SPANS):
+        send_far(d, 1)
+    arr[near_rows(0, q), :] = msg[1, rows(q), :]
 
     metas[1].wait_recv()
     metas[2].wait_recv()
@@ -204,10 +224,10 @@
         at = columns(d * span, span)
         for r in range(1, quarter):
             dnear1.append(go(send(
-                msg.at[2, rows(near(r)), at], arr.at[1, rows(q), at],
+                msg.at[2, rows(near(r)), at], arr.at[near_rows(1, q), at],
                 d1_s.at[d, r], d1_r.at[d, r], near_dev(r),
             )))
-    arr[1, rows(q), :] = msg[2, rows(q), :]
+    arr[near_rows(1, q), :] = msg[2, rows(q), :]
 
     def up(read, count):
         gu[...] = jnp.zeros_like(gu)
@@ -224,23 +244,23 @@
             gate / (1.0 + jnp.exp(-gate)) * gu[1, pl.ds(0, count), :]
         ).astype(BF16)
 
-    forwards = []
-
-    def forward(d):
-        at = columns(d * span, span)
-        for r in range(quarter):
-            dcross[d * quarter + r].wait_recv()
-            src = lax.rem(q + quarter - r, quarter)
-            forwards.append(go(send(
-                arr.at[2, rows(src), at], arr.at[3, rows(src), at],
+    forwards = [[], []]
+
+    def forward(d, b):
+        at = columns(d * span, span)
+        for r in range(b * group, (b + 1) * group):
+            dcross[d, r].wait_recv()
+            forwards[b].append(go(send(
+                arr.at[own_rows(r), at], arr.at[passed_rows(r), at],
                 fw_s.at[d, r], fw_r.at[d, r], ypart,
             )))
 
+    for d in range(SPANS):
+        forward(d, 0)
     shared_gu.wait()
     up(lambda at: jnp.concatenate([tok[0, 0, :, at], tok[1, 0, :, at]], axis=0), 2 * per)
     routed_gu = pltpu.make_async_copy(routed_w.at[0, pl.ds(0, 2)], wgu, load_sem.at[1])
     routed_gu.start()
-    forward(0)
     shared_d.wait()
 
     @pl.loop(0, width // STEP)
@@ -252,57 +272,65 @@
 
     routed_d = pltpu.make_async_copy(routed_w.at[0, 2], wd, load_sem.at[2])
     routed_d.start()
-    for d in range(1, SPANS):
-        forward(d)
-
-    for copy in dnear0 + dnear1 + forwards:
-        copy.wait_recv()
-    routed_gu.wait()
-    up(lambda at: arr[:, :, at].reshape(4 * nrow, DEPTH), 4 * nrow)
-    routed_d.wait()
 
     piece = width // PIECES
-    yreds, near0, near1, cross = [], [], [], []
-
-    def reduce(j):
-        yreds[j].wait_recv()
+    batch = 2 * nrow
+    yreds, near0, near1, cross = {}, [], [], {}
+    hrow = group * block
+
+    def reduce(b, j):
+        yreds[b, j].wait_recv()
         at = columns(j * piece, piece)
+        own = pl.ds(b * batch + nrow, hrow)
 
         @pl.loop(0, piece // STEP)
         def _(i):
             at = pl.ds(pl.multiple_of(j * piece + i * STEP, STEP), STEP)
-            part[2, :, at] = (part[2, :, at].astype(F32) + yred[:, at].astype(F32)).astype(BF16)
-
-        for r in range(quarter):
-            cross.append(go(send(
-                part.at[2, rows(near(r)), at], retc.at[rows(q), at],
-                rc_s.at[j, r], rc_r.at[j, r], far_dev(r),
+            part[own, at] = (
+                part[own, at].astype(F32) + yred[pl.ds(b * hrow, hrow), at].astype(F32)
+            ).astype(BF16)
+
+        for r in range(b * group, (b + 1) * group):
+            cross[j, r] = go(send(
+                part.at[own_rows(r), at], retc.at[rows(q), at],
+                rc_s.at[j, r], rc_r.at[j, r], back_dev(r),
+            ))
+
+    def down(b, j):
+        @pl.loop(0, piece // STEP)
+        def _(i):
+            at = pl.ds(pl.multiple_of(j * piece + i * STEP, STEP), STEP)
+            part[pl.ds(b * batch, batch), at] = dot_t(hid[...], wd[at, :]).astype(BF16)
+
+        at = columns(j * piece, piece)
+        yreds[b, j] = go(send(
+            part.at[pl.ds(b * batch + nrow + hrow, hrow), at], yred.at[pl.ds(b * hrow, hrow), at],
+            yr_s.at[b, j], yr_r.at[b, j], ypart,
+        ))
+        returned, s, r_ = (near0, r0_s, r0_r) if b == 0 else (near1, r1_s, r1_r)
+        for r in range(1, quarter):
+            returned.append(go(send(
+                part.at[near_rows(b, near(r)), at], rets.at[b, rows(q), at],
+                s.at[j, r], r_.at[j, r], near_dev(r),
             )))
 
-    for j in range(PIECES):
-        @pl.loop(0, piece // STEP)
-        def _(i):
-            at = pl.ds(pl.multiple_of(j * piece + i * STEP, STEP), STEP)
-            got = dot_t(hid[...], wd[at, :]).astype(BF16)
-            part[:, :, at] = got.reshape(4, nrow, STEP)
-
-        at = columns(j * piece, piece)
-        yreds.append(go(send(part.at[3, :, at], yred.at[:, at], yr_s.at[j], yr_r.at[j], ypart)))
-        for r in range(1, quarter):
-            near1.append(go(send(
-                part.at[1, rows(near(r)), at], rets.at[1, rows(q), at],
-                r1_s.at[j, r], r1_r.at[j, r], near_dev(r),
-            )))
-        for r in range(1, quarter):
-            near0.append(go(send(
-                part.at[0, rows(near(r)), at], rets.at[0, rows(q), at],
-                r0_s.at[j, r], r0_r.at[j, r], near_dev(r),
-            )))
-        if j > 0:
-            reduce(j - 1)
-    rets[0, rows(q), :] = part[0, rows(q), :]
-    rets[1, rows(q), :] = part[1, rows(q), :]
-    reduce(PIECES - 1)
+    for b in range(2):
+        for copy in (dnear0, dnear1)[b] + forwards[b]:
+            copy.wait_recv()
+        if b == 0:
+            routed_gu.wait()
+        up(lambda at: arr[pl.ds(b * batch, batch), at], batch)
+        if b == 0:
+            routed_d.wait()
+        for j in range(PIECES):
+            down(b, j)
+            if b == 0:
+                for d in range(j * SPANS // PIECES, (j + 1) * SPANS // PIECES):
+                    forward(d, 1)
+            if j > 0:
+                reduce(b, j - 1)
+        rets[b, rows(q), :] = part[near_rows(b, q), :]
+        reduce(b, PIECES - 1)
 
     sums = [[], []]
 
@@ -340,8 +368,8 @@
     for j in range(PIECES):
         for copy in near0[j * (quarter - 1) : (j + 1) * (quarter - 1)]:
             copy.wait_recv()
-        for copy in cross[j * quarter : (j + 1) * quarter]:
-            copy.wait_recv()
+        for r in range(quarter):
+            cross[j, r].wait_recv()
 
         @pl.loop(0, piece // STEP)
         def _(i):
@@ -392,13 +420,13 @@
         vmem((2 * per, nrow), BF16),
         vmem((2 * per, nrow), BF16),
         vmem((3, nrow, width), BF16),
-        vmem((4, nrow, width), BF16),
+        vmem((4 * nrow, width), BF16),
         vmem((2, width, hidden), BF16),
         vmem((width, hidden), BF16),
-        vmem((2, 4 * nrow, hidden), F32),
-        vmem((4 * nrow, hidden), BF16),
+        vmem((2, 2 * nrow, hidden), F32),
+        vmem((2 * nrow, hidden), BF16),
         vmem((2, per, width), BF16),
-        vmem((4, nrow, width), BF16),
+        vmem((4 * nrow, width), BF16),
         vmem((nrow, width), BF16),
         vmem((2, nrow, width), BF16),
         vmem((nrow, width), BF16),
@@ -411,7 +439,7 @@
     ]
     scratch += pair(4) + pair(SPANS) + pair(SPANS) + pair(SPANS)
     scratch += pair(SPANS, quarter) * 4
-    scratch += pair(PIECES) + pair(PIECES, quarter) * 3 + pair(2, PIECES) + pair(PIECES)
+    scratch += pair(2, PIECES) + pair(PIECES, quarter) * 3 + pair(2, PIECES) + pair(PIECES)
     return pl.pallas_call(
         functools.partial(kernel, experts),
         out_shape=jax.ShapeDtypeStruct((per, width), BF16),

time: 124 us -> 115 us (0.927)
  Pallas kernels: 121 us -> 112 us
    pallas_call x1, Pallas kernels: 121 us -> 112 us  [fused(): pl.pallas_call(functools.partial(kernel, experts), out_shape=jax.ShapeDty...]
where the time goes in v2:
time: 115 us; the launch traced here: 114 us
  Pallas kernels  112 us (97%)
  local copies, waits for them, and re-layouts  2.16 us (2%)
    pallas_call x1, Pallas kernels, fused(): pl.pallas_call(functools.partial(kernel, experts), out_shape=jax.ShapeDty...  112 us

profile of v2, /device:TPU:0, one launch (start us, length us, event | category | flops | bytes accessed | tf_op | source)
XLA Modules:
  0.0 114.5 jit_solution(5309937957361981943)
XLA Ops:
  0.0 112.3 %shard_map.55 = bf16[64,7168]{1,0:T(8,128)(2,1)} custom-call(bf16[64,7168]{1,0:T(8,128)(2,1)} %tokens.1, s32[8,64]{1,0:T(8,128)} %bitcast.2, s32[8,64]{1,0:T(8,128)} %bitcast.3, bf16[1,3,7168,512]{3,2,1,0:T(8,128)(2,1)} %routed_w.1, bf16[3,7168,512]{2,1,0:T(8,128)(2,1)} %shared_w.1), custom_call_target="tpu_custom_call" | custom-call | flops 8455716864 | bytes 44040192 | tf_op jit(solution)/shard_map/pallas_call | solution.py:443
  112.3 2.2 %copy.7 = bf16[64,7168]{1,0:T(8,128)(2,1)} copy(bf16[64,7168]{1,0:T(8,128)(2,1)} %shard_map.55) | data formatting | bytes 1835008
